TPU v7x, 32 devices: a whole 2x2x4 slice. The times are simulated.
32 devices in a mesh: sample: 2 (over y), gx: 16 (over z, x, core).
Axes of the slice: x: 2, y: 2, z: 4, core: 2. Of those that a mesh axis runs over, the one named last changes fastest.
Arguments:
- populations: float32 [19, 32, 128, 256], P(None, ('sample', 'gx')), parts along dimension 1, may hold values from 0.5 to 1.5
- solid_mask: int32 [32, 128, 256], P(('sample', 'gx')), parts along dimension 0, may hold values from 0 to 1, as said below
- relax_rates: float32 [19], replicated, may hold values from 0.7 to 1.9
- body_force: float32 [3], replicated, may hold values from -0.1 to 0.1
Outputs:
- final_populations: float32 [19, 32, 128, 256], P(None, ('sample', 'gx')), parts along dimension 1
There are 2 independent parts, one for each index of `sample`. A program takes and returns all parts, laid end to end along the dimension named above; an argument that names none is the same for every part. Nothing has to cross between parts.
Inputs may be any that keep to these rules, and one draw needn't show every extreme that they name: `solid_mask`: 1 marks a solid node, 0 a fluid node.
All inputs are finite; a program needn't handle non-finite values.
Results may differ from a plain program's by a relative error of at most 0.0003.
Values sent between devices are 32-bit elements; how exact they have to be, the bound alone decides.
A program may use at most 192 MiB of HBM per device.

v0:
```python
import jax
import jax.numpy as jnp
import numpy as np
from jax import lax
from jax.experimental import pallas as pl
from jax.experimental.pallas import tpu as pltpu
from jax.sharding import PartitionSpec as P

CHUNK_ROWS = 16
GROUP_ROWS = 8

VELOCITIES = [
    (0, 0, 0), (1, 0, 0), (-1, 0, 0), (0, 1, 0), (0, -1, 0), (0, 0, 1), (0, 0, -1),
    (1, 1, 0), (-1, -1, 0), (1, -1, 0), (-1, 1, 0), (1, 0, 1), (-1, 0, -1), (1, 0, -1),
    (-1, 0, 1), (0, 1, 1), (0, -1, -1), (0, 1, -1), (0, -1, 1),
]
OPPOSITE = [0, 2, 1, 4, 3, 6, 5, 8, 7, 10, 9, 12, 11, 14, 13, 16, 15, 18, 17]
LEVEL = [i for i in range(19) if VELOCITIES[i][0] == 0]
RISING = [i for i in range(19) if VELOCITIES[i][0] == 1]
FALLING = [i for i in range(19) if VELOCITIES[i][0] == -1]

EVEN_ROWS, EVEN_CLASS = (0, 7, 8, 9, 16, 17, 18), (0, 1, 3, 5, 7, 11, 15)
CROSS_ROWS = (4, 5, 6)
ODD_ROWS = ((1, 10, 11), (2, 12, 14), (3, 13, 15))
ODD_CLASS = ((1, 7, 11), (3, 7, 15), (5, 11, 15))


def moment_rows():
    c = np.array(VELOCITIES, np.float64)
    x, y, z = c[:, 0], c[:, 1], c[:, 2]
    polynomials = [
        np.ones(19), x, y, z, x * y, x * z, y * z, x**2, y**2, z**2, x * y**2, x * z**2,
        x**2 * y, x**2 * z, y * z**2, y**2 * z, x**2 * y**2, x**2 * z**2, y**2 * z**2,
    ]
    basis = []
    for row in polynomials:
        vector = row.copy()
        for earlier in basis:
            vector = vector - (vector @ earlier) / (earlier @ earlier) * earlier
        basis.append(vector)
    moments = np.stack(basis)
    return moments, np.sum(moments**2, axis=1)


MOMENTS, NORMS = moment_rows()


def kernel_entries():
    entries = {}
    for a in range(7):
        for b in range(a, 7):
            entries["even", a, b] = [
                (r, MOMENTS[r, EVEN_CLASS[a]] * MOMENTS[r, EVEN_CLASS[b]] / NORMS[r])
                for r in EVEN_ROWS
            ]
    for axis in range(3):
        for a in range(3):
            for b in range(a, 3):
                entries["odd", axis, a, b] = [
                    (
                        r,
                        MOMENTS[r, ODD_CLASS[axis][a]] * MOMENTS[r, ODD_CLASS[axis][b]] / NORMS[r],
                    )
                    for r in ODD_ROWS[axis]
                ]
    for k in range(3):
        entries["cross", k] = [(CROSS_ROWS[k], 1.0 / NORMS[CROSS_ROWS[k]])]
    return entries


ENTRIES = kernel_entries()
PLACE = {name: number for number, name in enumerate(ENTRIES)}


def fill_table(table, rates_ref):
    for name, terms in ENTRIES.items():
        total = None
        for r, factor in terms:
            if abs(factor) < 1e-12:
                continue
            term = rates_ref[r] * np.float32(factor)
            total = term if total is None else total + term
        table[PLACE[name]] = total if total is not None else jnp.float32(0.0)


def collide(f, solid, table, force):
    def even(a, b):
        return table[PLACE["even", min(a, b), max(a, b)]]

    def odd(axis, a, b):
        return table[PLACE["odd", axis, min(a, b), max(a, b)]]

    p = {i: f[i] + f[i + 1] for i in range(1, 19, 2)}
    d = {i: f[i] - f[i + 1] for i in range(1, 19, 2)}
    q_xy, q_xz, q_yz = p[7] + p[9], p[11] + p[13], p[15] + p[17]
    rho = f[0] + (p[1] + p[3] + p[5]) + (q_xy + q_xz + q_yz)
    x_parts = [d[1], d[7] + d[9], d[11] + d[13]]
    y_parts = [d[3], d[7] - d[9], d[15] + d[17]]
    z_parts = [d[5], d[11] - d[13], d[15] - d[17]]
    parts = [x_parts, y_parts, z_parts]
    j = [v[0] + v[1] + v[2] for v in parts]
    inverse = 1.0 / rho
    u = [v * inverse for v in j]
    xx, yy, zz = j[0] * u[0], j[1] * u[1], j[2] * u[2]
    square = xx + yy + zz
    third = 1.0 / 3.0
    base = rho * (1.0 / 9.0) - square * (1.0 / 6.0)
    e = [
        f[0] - (rho * third - 0.5 * square),
        p[1] - (base + 0.5 * xx),
        p[3] - (base + 0.5 * yy),
        p[5] - (base + 0.5 * zz),
        q_xy - (base + 0.5 * (xx + yy)),
        q_xz - (base + 0.5 * (xx + zz)),
        q_yz - (base + 0.5 * (yy + zz)),
    ]
    cross = [
        table[PLACE["cross", 0]] * ((p[7] - p[9]) - j[0] * u[1]),
        table[PLACE["cross", 1]] * ((p[11] - p[13]) - j[0] * u[2]),
        table[PLACE["cross", 2]] * ((p[15] - p[17]) - j[1] * u[2]),
    ]
    even_out = []
    for a in range(7):
        total = even(a, 0) * e[0]
        for b in range(1, 7):
            total = total + even(a, b) * e[b]
        even_out.append(total)
    odd_out = []
    for axis in range(3):
        share = j[axis] * third
        n = [v - share for v in parts[axis]]
        out = []
        for a in range(3):
            total = odd(axis, a, 0) * n[0] + odd(axis, a, 1) * n[1] + odd(axis, a, 2) * n[2]
            push = force[axis] * np.float32(1.0 / 6.0 if a == 0 else 1.0 / 12.0)
            out.append(push * rho - total)
        odd_out.append(out)
    (x1, x_xy, x_xz), (y1, y_xy, y_yz), (z1, z_xz, z_yz) = odd_out
    even_part = {
        1: even_out[1], 3: even_out[2], 5: even_out[3],
        7: even_out[4] + cross[0], 9: even_out[4] - cross[0],
        11: even_out[5] + cross[1], 13: even_out[5] - cross[1],
        15: even_out[6] + cross[2], 17: even_out[6] - cross[2],
    }
    odd_part = {
        1: x1, 3: y1, 5: z1, 7: x_xy + y_xy, 9: x_xy - y_xy,
        11: x_xz + z_xz, 13: x_xz - z_xz, 15: y_yz + z_yz, 17: y_yz - z_yz,
    }
    relaxed = [jnp.where(solid, f[0], f[0] - even_out[0])]
    for i in range(1, 19, 2):
        relaxed.append(jnp.where(solid, f[i + 1], (f[i] - even_part[i]) + odd_part[i]))
        relaxed.append(jnp.where(solid, f[i], (f[i + 1] - even_part[i]) - odd_part[i]))
    return relaxed


def slot(i, level, moving):
    if i in LEVEL:
        return level.at[LEVEL.index(i)]
    if i in RISING:
        return moving.at[0, RISING.index(i)]
    return moving.at[1, FALLING.index(i)]


def steps_kernel(
    pops_ref, mask_ref, rates_ref, force_ref, level_out, moving_out,
    pops, mask, level1, send1, recv1, level2, send2, table,
    pops_sem, mask_sem, send_sem, recv_sem, out_sem,
):
    count = lax.axis_size("gx")
    me = lax.axis_index("gx")
    targets = (lax.rem(me + 1, count), lax.rem(me + count - 1, count))
    height, breadth = mask.shape
    chunks = height // CHUNK_ROWS

    def rows(c):
        return pl.ds(pl.multiple_of(c * CHUNK_ROWS, CHUNK_ROWS), CHUNK_ROWS)

    def bring_pops(c):
        return pltpu.make_async_copy(
            pops_ref.at[:, rows(c), :], pops.at[:, rows(c), :], pops_sem.at[c]
        )

    bring_mask = pltpu.make_async_copy(mask_ref, mask, mask_sem)

    def ship(turn, way, c):
        source, target = (send1, recv1) if turn == 0 else (send2, moving_out)
        return pltpu.make_async_remote_copy(
            src_ref=source.at[way, :, rows(c), :],
            dst_ref=target.at[way, :, rows(c), :],
            send_sem=send_sem.at[turn, way, c],
            recv_sem=recv_sem.at[turn, way, c],
            device_id={"gx": targets[way]},
            device_id_type=pl.DeviceIdType.MESH,
        )

    def put_level(c):
        return pltpu.make_async_copy(
            level2.at[:, rows(c), :], level_out.at[:, rows(c), :], out_sem.at[c]
        )

    bring_pops(chunks - 1).start()
    bring_mask.start()

    @pl.loop(0, chunks - 1)
    def _(c):
        bring_pops(c).start()

    barrier = pltpu.get_barrier_semaphore()
    for target in targets:
        pl.semaphore_signal(
            barrier, inc=1, device_id={"gx": target}, device_id_type=pl.DeviceIdType.MESH
        )
    fill_table(table, rates_ref)
    force = [force_ref[axis] for axis in range(3)]

    row = lax.broadcasted_iota(jnp.int32, (GROUP_ROWS, breadth), 0)

    def work(c, load, level, moving):
        for part in range(CHUNK_ROWS // GROUP_ROWS):
            start = pl.multiple_of(c * CHUNK_ROWS + part * GROUP_ROWS, GROUP_ROWS)
            here = pl.ds(start, GROUP_ROWS)
            f = [load(i, here) for i in range(19)]
            relaxed = collide(f, mask[here, :] == 1, table, force)
            for i in range(19):
                _, along_y, along_z = VELOCITIES[i]
                value, plane = relaxed[i], slot(i, level, moving)
                if along_z:
                    value = pltpu.roll(value, along_z % breadth, 1)
                if not along_y:
                    plane[here, :] = value
                    continue
                value = pltpu.roll(value, along_y % GROUP_ROWS, 0)
                beyond = lax.rem(start + (height + along_y * GROUP_ROWS), height)
                beyond = pl.ds(pl.multiple_of(beyond, GROUP_ROWS), GROUP_ROWS)
                crosses = row == (0 if along_y == 1 else GROUP_ROWS - 1)
                pltpu.store(plane.at[here, :], value, mask=jnp.logical_not(crosses))
                pltpu.store(plane.at[beyond, :], value, mask=crosses)

    bring_mask.wait()

    @pl.loop(0, chunks)
    def _(t):
        c = lax.rem(t + (chunks - 1), chunks)
        bring_pops(c).wait()
        work(c, lambda i, here: pops[i, here, :], level1, send1)

        @pl.when(t == 1)
        def _():
            pl.semaphore_wait(barrier, 2)

        @pl.when(t >= 2)
        def _():
            for way in range(2):
                ship(0, way, t - 2).start()

    for c in (chunks - 2, chunks - 1):
        for way in range(2):
            ship(0, way, c).start()

    def arrived(i, here):
        if i in LEVEL:
            return level1[LEVEL.index(i), here, :]
        return slot(i, None, recv1)[here, :]

    @pl.loop(0, chunks)
    def _(c):
        for way in range(2):
            ship(0, way, c).wait_recv()
        work(c, arrived, level2, send2)

        @pl.when(c >= 2)
        def _():
            for way in range(2):
                ship(1, way, c - 1).start()
            put_level(c - 1).start()

    for c in (chunks - 1, 0):
        for way in range(2):
            ship(1, way, c).start()
        put_level(c).start()

    @pl.loop(0, chunks)
    def _(c):
        for way in range(2):
            ship(0, way, c).wait_send()
            ship(1, way, c).wait_send()
            ship(1, way, c).wait_recv()
        put_level(c).wait()


def place_kernel(level_ref, moving_ref, out_ref, sems):
    copies = [
        pltpu.make_async_copy(slot(i, level_ref, moving_ref), out_ref.at[i], sems.at[i])
        for i in range(19)
    ]
    for copy in copies:
        copy.start()
    for copy in copies:
        copy.wait()


def on_device(populations, solid_mask, relax_rates, body_force):
    channels, depth, height, breadth = populations.shape
    chunks = height // CHUNK_ROWS
    f32 = jnp.float32
    anywhere = pl.BlockSpec(memory_space=pl.ANY)
    in_hbm = pl.BlockSpec(memory_space=pltpu.HBM)
    scalars = pl.BlockSpec(memory_space=pltpu.SMEM)
    level, moving = pl.pallas_call(
        steps_kernel,
        out_shape=(
            jax.ShapeDtypeStruct((len(LEVEL), height, breadth), f32),
            jax.ShapeDtypeStruct((2, len(RISING), height, breadth), f32),
        ),
        in_specs=[in_hbm, in_hbm, scalars, scalars],
        out_specs=(anywhere, anywhere),
        scratch_shapes=[
            pltpu.VMEM((channels, height, breadth), f32),
            pltpu.VMEM((height, breadth), jnp.int32),
            pltpu.VMEM((len(LEVEL), height, breadth), f32),
            pltpu.VMEM((2, len(RISING), height, breadth), f32),
            pltpu.VMEM((2, len(RISING), height, breadth), f32),
            pltpu.VMEM((len(LEVEL), height, breadth), f32),
            pltpu.VMEM((2, len(RISING), height, breadth), f32),
            pltpu.SMEM((len(ENTRIES),), f32),
            pltpu.SemaphoreType.DMA((chunks,)),
            pltpu.SemaphoreType.DMA,
            pltpu.SemaphoreType.DMA((2, 2, chunks)),
            pltpu.SemaphoreType.DMA((2, 2, chunks)),
            pltpu.SemaphoreType.DMA((chunks,)),
        ],
        compiler_params=pltpu.CompilerParams(
            collective_id=0, has_side_effects=True, vmem_limit_bytes=32 * 1024 * 1024
        ),
    )(
        populations.reshape(channels, height, breadth),
        solid_mask.reshape(height, breadth),
        relax_rates,
        body_force,
    )
    placed = pl.pallas_call(
        place_kernel,
        out_shape=jax.ShapeDtypeStruct((channels, height, breadth), f32),
        in_specs=[anywhere, anywhere],
        out_specs=in_hbm,
        scratch_shapes=[pltpu.SemaphoreType.DMA((channels,))],
        compiler_params=pltpu.CompilerParams(vmem_limit_bytes=1024 * 1024),
    )(level, moving)
    return placed.reshape(populations.shape)


def solution(mesh):
    in_specs = (P(None, ("sample", "gx"), None, None), P(("sample", "gx"), None, None), P(), P())
    out_specs = P(None, ("sample", "gx"), None, None)
    return jax.shard_map(
        on_device, mesh=mesh, in_specs=in_specs, out_specs=out_specs, check_vma=False
    )
```

profile of v0, /device:TPU:1, one launch (start us, length us, event | category | flops | bytes accessed | tf_op | source)
XLA Modules:
  0.0 40.2 jit_solution(17593180210043291749)
XLA Ops:
  0.0 0.0 copy-start
  0.0 1.7 %copy-done = f32[19,1,128,256]{3,2,1,0:T(8,128)S(1)} copy-done((f32[19,1,128,256]{3,2,1,0:T(8,128)S(1)}, f32[19,1,128,256]{3,2,1,0:T(8,128)}, u32[]{:S(2)}) %copy-start) | copy-done | bytes 2490392
  1.7 0.0 copy-start.1
  1.7 0.9 %copy-done.1 = s32[1,128,256]{2,1,0:T(8,128)S(1)} copy-done((s32[1,128,256]{2,1,0:T(8,128)S(1)}, s32[1,128,256]{2,1,0:T(8,128)}, u32[]{:S(2)}) %copy-start.1) | copy-done | bytes 131096
  2.6 0.0 copy-start.2
  2.6 0.7 %copy-done.2 = f32[19]{0:T(128)S(1)} copy-done((f32[19]{0:T(128)S(1)}, f32[19]{0:T(128)}, u32[]{:S(2)}) %copy-start.2) | copy-done | bytes 100
  3.3 0.0 copy-start.3
  3.3 0.7 %copy-done.3 = f32[3]{0:T(128)S(1)} copy-done((f32[3]{0:T(128)S(1)}, f32[3]{0:T(128)}, u32[]{:S(2)}) %copy-start.3) | copy-done | bytes 36
  3.9 34.6 %shard_map.46 = (f32[9,128,256]{2,1,0:T(8,128)S(1)}, f32[2,5,128,256]{3,2,1,0:T(8,128)S(1)}) custom-call(f32[19,128,256]{2,1,0:T(8,128)S(1)} %bitcast.5, s32[128,256]{1,0:T(8,128)S(1)} %bitcast.6, f32[19]{0:T(128)S(1)} %copy-done.2, f32[3]{0:T(128)S(1)} %copy-done.3), custom_call_target="tpu_custom_call" | custom-call | tf_op jit(solution)/shard_map/pallas_call | solution.py:309
  38.6 1.6 %shard_map.47 = f32[19,128,256]{2,1,0:T(8,128)} custom-call(f32[9,128,256]{2,1,0:T(8,128)S(1)} %get-tuple-element.7.level_ref, f32[2,5,128,256]{3,2,1,0:T(8,128)S(1)} %get-tuple-element.8.moving_ref), custom_call_target="tpu_custom_call" | custom-call | tf_op jit(solution)/shard_map/pallas_call | solution.py:341
Async XLA Ops:
  0.0 1.7 %copy-start = (f32[19,1,128,256]{3,2,1,0:T(8,128)S(1)}, f32[19,1,128,256]{3,2,1,0:T(8,128)}, u32[]{:S(2)}) copy-start(f32[19,1,128,256]{3,2,1,0:T(8,128)} %param.4) | copy-start | bytes 7471108
  1.7 0.9 %copy-start.1 = (s32[1,128,256]{2,1,0:T(8,128)S(1)}, s32[1,128,256]{2,1,0:T(8,128)}, u32[]{:S(2)}) copy-start(s32[1,128,256]{2,1,0:T(8,128)} %param.5) | copy-start | bytes 393220
  2.6 0.7 %copy-start.2 = (f32[19]{0:T(128)S(1)}, f32[19]{0:T(128)}, u32[]{:S(2)}) copy-start(f32[19]{0:T(128)} %rates_ref.1) | copy-start | bytes 232
  3.3 0.7 %copy-start.3 = (f32[3]{0:T(128)S(1)}, f32[3]{0:T(128)}, u32[]{:S(2)}) copy-start(f32[3]{0:T(128)} %force_ref.1) | copy-start | bytes 40
where the time goes:
time: 40.3 us; the launch traced here: 40.2 us
  Pallas kernels  36.2 us (90%)
  local copies, waits for them, and re-layouts  3.92 us (10%)
    pallas_call x1, Pallas kernels, on_device(): pl.pallas_call(steps_kernel, out_shape=(jax.ShapeDtypeStruct((len(LEVEL),...  34.6 us
    unnamed x8, local copies, waits for them, and re-layouts  3.92 us
    pallas_call x1, Pallas kernels, on_device(): pl.pallas_call(place_kernel, out_shape=jax.ShapeDtypeStruct((channels, he...  1.6 us

commit v1 on v0

--- a/solution.py
+++ b/solution.py
@@ -162,9 +162,9 @@
 
 
 def steps_kernel(
-    pops_ref, mask_ref, rates_ref, force_ref, level_out, moving_out,
-    pops, mask, level1, send1, recv1, level2, send2, table,
-    pops_sem, mask_sem, send_sem, recv_sem, out_sem,
+    pops_ref, mask_ref, rates_hbm, force_hbm, level_out, moving_out,
+    rates_ref, force_ref, pops, mask, level1, send1, recv1, level2, send2, table,
+    scalar_sem, pops_sem, mask_sem, send_sem, recv_sem, out_sem,
 ):
     count = lax.axis_size("gx")
     me = lax.axis_index("gx")
@@ -198,6 +198,12 @@
             level2.at[:, rows(c), :], level_out.at[:, rows(c), :], out_sem.at[c]
         )
 
+    bring_scalars = (
+        pltpu.make_async_copy(rates_hbm, rates_ref, scalar_sem.at[0]),
+        pltpu.make_async_copy(force_hbm, force_ref, scalar_sem.at[1]),
+    )
+    for bring in bring_scalars:
+        bring.start()
     bring_pops(chunks - 1).start()
     bring_mask.start()
 
@@ -210,6 +216,8 @@
         pl.semaphore_signal(
             barrier, inc=1, device_id={"gx": target}, device_id_type=pl.DeviceIdType.MESH
         )
+    for bring in bring_scalars:
+        bring.wait()
     fill_table(table, rates_ref)
     force = [force_ref[axis] for axis in range(3)]
 
@@ -305,16 +313,17 @@
     f32 = jnp.float32
     anywhere = pl.BlockSpec(memory_space=pl.ANY)
     in_hbm = pl.BlockSpec(memory_space=pltpu.HBM)
-    scalars = pl.BlockSpec(memory_space=pltpu.SMEM)
     level, moving = pl.pallas_call(
         steps_kernel,
         out_shape=(
             jax.ShapeDtypeStruct((len(LEVEL), height, breadth), f32),
             jax.ShapeDtypeStruct((2, len(RISING), height, breadth), f32),
         ),
-        in_specs=[in_hbm, in_hbm, scalars, scalars],
+        in_specs=[in_hbm] * 4,
         out_specs=(anywhere, anywhere),
         scratch_shapes=[
+            pltpu.SMEM(relax_rates.shape, f32),
+            pltpu.SMEM(body_force.shape, f32),
             pltpu.VMEM((channels, height, breadth), f32),
             pltpu.VMEM((height, breadth), jnp.int32),
             pltpu.VMEM((len(LEVEL), height, breadth), f32),
@@ -323,6 +332,7 @@
             pltpu.VMEM((len(LEVEL), height, breadth), f32),
             pltpu.VMEM((2, len(RISING), height, breadth), f32),
             pltpu.SMEM((len(ENTRIES),), f32),
+            pltpu.SemaphoreType.DMA((2,)),
             pltpu.SemaphoreType.DMA((chunks,)),
             pltpu.SemaphoreType.DMA,
             pltpu.SemaphoreType.DMA((2, 2, chunks)),
@@ -333,10 +343,10 @@
             collective_id=0, has_side_effects=True, vmem_limit_bytes=32 * 1024 * 1024
         ),
     )(
-        populations.reshape(channels, height, breadth),
-        solid_mask.reshape(height, breadth),
-        relax_rates,
-        body_force,
+        pltpu.with_memory_space_constraint(populations.reshape(channels, height, breadth), pltpu.HBM),
+        pltpu.with_memory_space_constraint(solid_mask.reshape(height, breadth), pltpu.HBM),
+        pltpu.with_memory_space_constraint(relax_rates, pltpu.HBM),
+        pltpu.with_memory_space_constraint(body_force, pltpu.HBM),
     )
     placed = pl.pallas_call(
         place_kernel,

time: 40.3 us -> 36.3 us (0.901)
  local copies, waits for them, and re-layouts: 3.92 us -> 0 us
    unnamed x8 -> x0, local copies, waits for them, and re-layouts: 3.92 us -> none
where the time goes in v1:
time: 36.3 us; the launch traced here: 36.2 us
  Pallas kernels  36.2 us (100%)
    pallas_call x1, Pallas kernels, on_device(): pl.pallas_call(steps_kernel, out_shape=(jax.ShapeDtypeStruct((len(LEVEL),...  34.6 us
    pallas_call x1, Pallas kernels, on_device(): pl.pallas_call(place_kernel, out_shape=jax.ShapeDtypeStruct((channels, he...  1.6 us

profile of v1, /device:TPU:1, one launch (start us, length us, event | category | flops | bytes accessed | tf_op | source)
XLA Modules:
  0.0 36.2 jit_solution(2338338884070630283)
XLA Ops:
  0.0 34.6 %shard_map.46 = (f32[9,128,256]{2,1,0:T(8,128)S(1)}, f32[2,5,128,256]{3,2,1,0:T(8,128)S(1)}) custom-call(f32[19,128,256]{2,1,0:T(8,128)} %bitcast.5, s32[128,256]{1,0:T(8,128)} %bitcast.6, f32[19]{0:T(128)} %rates_hbm.1, f32[3]{0:T(128)} %force_hbm.1), custom_call_target="tpu_custom_call" | custom-call | tf_op jit(solution)/shard_map/pallas_call | solution.py:316
  34.6 1.6 %shard_map.47 = f32[19,128,256]{2,1,0:T(8,128)} custom-call(f32[9,128,256]{2,1,0:T(8,128)S(1)} %get-tuple-element.7.level_ref, f32[2,5,128,256]{3,2,1,0:T(8,128)S(1)} %get-tuple-element.8.moving_ref), custom_call_target="tpu_custom_call" | custom-call | tf_op jit(solution)/shard_map/pallas_call | solution.py:351

commit v2 on v1

--- a/solution.py
+++ b/solution.py
@@ -168,16 +168,21 @@
 ):
     count = lax.axis_size("gx")
     me = lax.axis_index("gx")
+    ways = (lax.rem(me + 1, 2), lax.rem(me, 2))
     targets = (lax.rem(me + 1, count), lax.rem(me + count - 1, count))
     height, breadth = mask.shape
-    chunks = height // CHUNK_ROWS
+    chunks, groups = height // CHUNK_ROWS, height // GROUP_ROWS
+    each = CHUNK_ROWS // GROUP_ROWS
 
     def rows(c):
         return pl.ds(pl.multiple_of(c * CHUNK_ROWS, CHUNK_ROWS), CHUNK_ROWS)
 
-    def bring_pops(c):
+    def group_rows(g):
+        return pl.ds(pl.multiple_of(g * GROUP_ROWS, GROUP_ROWS), GROUP_ROWS)
+
+    def bring_pops(g):
         return pltpu.make_async_copy(
-            pops_ref.at[:, rows(c), :], pops.at[:, rows(c), :], pops_sem.at[c]
+            pops_ref.at[:, group_rows(g), :], pops.at[:, group_rows(g), :], pops_sem.at[g]
         )
 
     bring_mask = pltpu.make_async_copy(mask_ref, mask, mask_sem)
@@ -189,7 +194,7 @@
             dst_ref=target.at[way, :, rows(c), :],
             send_sem=send_sem.at[turn, way, c],
             recv_sem=recv_sem.at[turn, way, c],
-            device_id={"gx": targets[way]},
+            device_id={"gx": lax.rem(me + 1 + way * (count - 2), count)},
             device_id_type=pl.DeviceIdType.MESH,
         )
 
@@ -198,24 +203,25 @@
             level2.at[:, rows(c), :], level_out.at[:, rows(c), :], out_sem.at[c]
         )
 
+    barrier = pltpu.get_barrier_semaphore()
+    for target in targets:
+        pl.semaphore_signal(
+            barrier, inc=1, device_id={"gx": target}, device_id_type=pl.DeviceIdType.MESH
+        )
     bring_scalars = (
         pltpu.make_async_copy(rates_hbm, rates_ref, scalar_sem.at[0]),
         pltpu.make_async_copy(force_hbm, force_ref, scalar_sem.at[1]),
     )
     for bring in bring_scalars:
         bring.start()
-    bring_pops(chunks - 1).start()
+    bring_pops(groups - 1).start()
+    bring_pops(0).start()
     bring_mask.start()
 
-    @pl.loop(0, chunks - 1)
-    def _(c):
-        bring_pops(c).start()
-
-    barrier = pltpu.get_barrier_semaphore()
-    for target in targets:
-        pl.semaphore_signal(
-            barrier, inc=1, device_id={"gx": target}, device_id_type=pl.DeviceIdType.MESH
-        )
+    @pl.loop(1, groups - 1)
+    def _(g):
+        bring_pops(g).start()
+
     for bring in bring_scalars:
         bring.wait()
     fill_table(table, rates_ref)
@@ -223,9 +229,9 @@
 
     row = lax.broadcasted_iota(jnp.int32, (GROUP_ROWS, breadth), 0)
 
-    def work(c, load, level, moving):
-        for part in range(CHUNK_ROWS // GROUP_ROWS):
-            start = pl.multiple_of(c * CHUNK_ROWS + part * GROUP_ROWS, GROUP_ROWS)
+    def work(numbers, load, level, moving):
+        for g in numbers:
+            start = pl.multiple_of(g * GROUP_ROWS, GROUP_ROWS)
             here = pl.ds(start, GROUP_ROWS)
             f = [load(i, here) for i in range(19)]
             relaxed = collide(f, mask[here, :] == 1, table, force)
@@ -248,22 +254,22 @@
 
     @pl.loop(0, chunks)
     def _(t):
-        c = lax.rem(t + (chunks - 1), chunks)
-        bring_pops(c).wait()
-        work(c, lambda i, here: pops[i, here, :], level1, send1)
-
-        @pl.when(t == 1)
+        numbers = [lax.rem(t * each + (groups - 1 + k), groups) for k in range(each)]
+        for g in numbers:
+            bring_pops(g).wait()
+        work(numbers, lambda i, here: pops[i, here, :], level1, send1)
+
+        @pl.when(t == 0)
         def _():
             pl.semaphore_wait(barrier, 2)
 
-        @pl.when(t >= 2)
+        @pl.when(t >= 1)
         def _():
-            for way in range(2):
-                ship(0, way, t - 2).start()
-
-    for c in (chunks - 2, chunks - 1):
-        for way in range(2):
-            ship(0, way, c).start()
+            for way in ways:
+                ship(0, way, t - 1).start()
+
+    for way in ways:
+        ship(0, way, chunks - 1).start()
 
     def arrived(i, here):
         if i in LEVEL:
@@ -274,16 +280,16 @@
     def _(c):
         for way in range(2):
             ship(0, way, c).wait_recv()
-        work(c, arrived, level2, send2)
+        work([c * each + k for k in range(each)], arrived, level2, send2)
 
         @pl.when(c >= 2)
         def _():
-            for way in range(2):
+            for way in ways:
                 ship(1, way, c - 1).start()
             put_level(c - 1).start()
 
     for c in (chunks - 1, 0):
-        for way in range(2):
+        for way in ways:
             ship(1, way, c).start()
         put_level(c).start()
 
@@ -297,9 +303,19 @@
 
 
 def place_kernel(level_ref, moving_ref, out_ref, sems):
+    moves = [(moving_ref.at[0, k], out_ref.at[i]) for k, i in enumerate(RISING)]
+    moves += [(moving_ref.at[1, k], out_ref.at[i]) for k, i in enumerate(FALLING)]
+    first = 0
+    while first < len(LEVEL):
+        last = first
+        while last + 1 < len(LEVEL) and LEVEL[last + 1] == LEVEL[last] + 1:
+            last += 1
+        size = last - first + 1
+        moves.append((level_ref.at[pl.ds(first, size)], out_ref.at[pl.ds(LEVEL[first], size)]))
+        first = last + 1
     copies = [
-        pltpu.make_async_copy(slot(i, level_ref, moving_ref), out_ref.at[i], sems.at[i])
-        for i in range(19)
+        pltpu.make_async_copy(source, target, sems.at[k])
+        for k, (source, target) in enumerate(moves)
     ]
     for copy in copies:
         copy.start()
@@ -333,7 +349,7 @@
             pltpu.VMEM((2, len(RISING), height, breadth), f32),
             pltpu.SMEM((len(ENTRIES),), f32),
             pltpu.SemaphoreType.DMA((2,)),
-            pltpu.SemaphoreType.DMA((chunks,)),
+            pltpu.SemaphoreType.DMA((height // GROUP_ROWS,)),
             pltpu.SemaphoreType.DMA,
             pltpu.SemaphoreType.DMA((2, 2, chunks)),
             pltpu.SemaphoreType.DMA((2, 2, chunks)),

time: 36.3 us -> 36.2 us (level)
  no operation moved by 1% of the time
where the time goes in v2:
time: 36.2 us; the launch traced here: 36.1 us
  Pallas kernels  36.1 us (100%)
    pallas_call x1, Pallas kernels, on_device(): pl.pallas_call(steps_kernel, out_shape=(jax.ShapeDtypeStruct((len(LEVEL),...  34.4 us
    pallas_call x1, Pallas kernels, on_device(): pl.pallas_call(place_kernel, out_shape=jax.ShapeDtypeStruct((channels, he...  1.61 us

profile of v2, /device:TPU:1, one launch (start us, length us, event | category | flops | bytes accessed | tf_op | source)
XLA Modules:
  0.0 36.1 jit_solution(9873304359268765366)
XLA Ops:
  0.0 34.4 %shard_map.46 = (f32[9,128,256]{2,1,0:T(8,128)S(1)}, f32[2,5,128,256]{3,2,1,0:T(8,128)S(1)}) custom-call(f32[19,128,256]{2,1,0:T(8,128)} %bitcast.5, s32[128,256]{1,0:T(8,128)} %bitcast.6, f32[19]{0:T(128)} %rates_hbm.1, f32[3]{0:T(128)} %force_hbm.1), custom_call_target="tpu_custom_call" | custom-call | tf_op jit(solution)/shard_map/pallas_call | solution.py:332
  34.5 1.6 %shard_map.47 = f32[19,128,256]{2,1,0:T(8,128)} custom-call(f32[9,128,256]{2,1,0:T(8,128)S(1)} %get-tuple-element.7.level_ref, f32[2,5,128,256]{3,2,1,0:T(8,128)S(1)} %get-tuple-element.8.moving_ref), custom_call_target="tpu_custom_call" | custom-call | tf_op jit(solution)/shard_map/pallas_call | solution.py:367
